TPU v7x, 32 devices: a whole 2x2x4 slice. The times are simulated.
32 devices in a mesh: ka: 2 (over x), gy: 4 (over z), gz: 4 (over y, core).
Axes of the slice: x: 2, y: 2, z: 4, core: 2. Of those that a mesh axis runs over, the one named last changes fastest.
Arguments:
- loads: float32 [32, 3, 128, 512], P('ka', None, 'gy', 'gz'), may hold values from -1 to 1
- sleeper_pos: int32 [32], P('ka'), may hold values from 0 to 127
- material: int32 [128, 512], P('gy', 'gz'), may hold values from 0 to 7, as said below
- material_table: float32 [8, 8], replicated, may hold values from -1 to 3, as said below
Outputs:
- adjoint_field: float32 [128, 2, 3, 128, 512], P('ka', None, None, 'gy', 'gz')
Inputs may be any that keep to these rules, and one draw needn't show every extreme that they name: layered: the material index never falls with depth in a column, layer boundaries vary from column to column, and every material occurs. `material_table`: shifts and damping positive, each material's coupling matrix diagonally dominant with a positive diagonal.
All inputs are finite; a program needn't handle non-finite values.
Results may differ from a plain program's by a relative error of at most 0.0002.
Values sent between devices are 32-bit elements; how exact they have to be, the bound alone decides.
No kernel may reach another device: no remote copies, remote signals or barrier semaphores. Data moves between devices by JAX's collectives and lax.ppermute only.
A program may use at most 128 MiB of HBM per device.

v0:
```python
import functools
import math

import jax
import jax.numpy as jnp
from jax import lax
from jax.experimental import pallas as pl
from jax.experimental.pallas import tpu as pltpu
from jax.sharding import PartitionSpec as P

KW = 128
NMAT = 8
DEG = 4
LANES = 128
HALF = 64
SEGS = 16
HY = 7
HB = 8


def lanes_for(sleepers):
    return -(-(3 * sleepers + 3 * NMAT) // LANES) * LANES


def two_parts(values):
    high = values.astype(jnp.bfloat16)
    low = (values - high.astype(jnp.float32)).astype(jnp.bfloat16)
    return high, low


def dot(a, b):
    return lax.dot_general(a, b, (((1,), (0,)), ((), ())), preferred_element_type=jnp.float32)


def dot_t(a, b):
    return lax.dot_general(a, b, (((1,), (1,)), ((), ())), preferred_element_type=jnp.float32)


def table_kernel(sleepers, count, start, table, cells, positions, tw, tc, vectors):
    width = tc.shape[0] // 2
    lane = lax.broadcasted_iota(jnp.int32, (8, LANES), 1)
    wave = lane % HALF
    live = wave < count
    wave = wave + start[0]
    q = (2.0 * jnp.sin(wave.astype(jnp.float32) * (math.pi / KW))) ** 2
    lowest = highest = None
    for m in range(NMAT):
        s, xx, yy, zz, xy, xz, yz = (jnp.full((8, LANES), table[m, f]) for f in range(7))
        xy, xz, yz = jnp.abs(xy), jnp.abs(xz), jnp.abs(yz)
        sums = (xy + xz, xy + yz, xz + yz)
        low = s + q * functools.reduce(jnp.minimum, [d - r for d, r in zip((xx, yy, zz), sums)])
        high = s + q * functools.reduce(jnp.maximum, [d + r for d, r in zip((xx, yy, zz), sums)])
        lowest = low if m == 0 else jnp.minimum(lowest, low)
        highest = high if m == 0 else jnp.maximum(highest, high)
    highest = 8.0 + highest
    center = 0.5 * (highest + lowest)
    half_width = 0.5 * (highest - lowest)
    ratio2 = (center / half_width) ** 2
    top = 8.0 * ratio2 * (ratio2 - 1.0) + 1.0
    h2 = half_width * half_width
    h4 = h2 * h2
    scale = 8.0 / (top * h4)
    scale = jnp.where(live, scale * scale, 0.0)
    for n, vector in enumerate((-h2, (top + 1.0) * h4 * 0.125, lowest * highest, center)):
        vectors[n, :, :] = jnp.where(live, vector, 0.0)

    tc[...] = jnp.zeros(tc.shape, jnp.bfloat16)
    tw[...] = jnp.zeros(tw.shape, jnp.bfloat16)
    column = [jnp.broadcast_to(cells[:, f : f + 1], (8, LANES)) for f in range(8)]
    fields = [center - 4.0 - column[0] - q * column[c] for c in (1, 2, 3)]
    fields += [-q * column[c] for c in (4, 5, 6)] + [q * column[7]]
    rounded = lambda values: values.astype(jnp.bfloat16).astype(jnp.float32)
    for f, field in enumerate(fields):
        field = jnp.where(live, field, 0.0)
        first = rounded(field)
        second = rounded(field - first)
        third = field - first - second
        rows = jnp.concatenate([first, second, third, jnp.zeros_like(first)], axis=0)
        lanes = lax.broadcasted_iota(jnp.int32, rows.shape, 1)
        for half in range(2):
            kept = jnp.where(lanes // HALF == half, rows, 0.0).astype(jnp.bfloat16)
            at = half * width + 3 * sleepers
            tc[at : at + 32, f * LANES : (f + 1) * LANES] = kept

    turns = (positions[...] * wave[:1]) & (KW - 1)
    angles = turns.astype(jnp.float32) * (2.0 * math.pi / KW)
    lanes = lax.broadcasted_iota(jnp.int32, turns.shape, 1)
    for part, phase in enumerate((jnp.cos(angles), -jnp.sin(angles))):
        phase = phase * scale[:1]
        high = rounded(phase)
        for segment, values in enumerate((high, high, phase - high)):
            for half in range(2):
                kept = jnp.where(lanes // HALF == half, values, 0.0).astype(jnp.bfloat16)
                for c in range(3):
                    at = (2 * segment + half) * width + c * sleepers
                    to = (2 * c + part) * LANES
                    tw[at : at + sleepers, to : to + LANES] = kept


def tables(positions, material_table, start, count, width):
    sleepers = positions.shape[0]
    spots = jnp.broadcast_to(positions[:, None], (sleepers, LANES))
    return pl.pallas_call(
        functools.partial(table_kernel, sleepers, count),
        out_shape=(
            jax.ShapeDtypeStruct((6 * width, 6 * LANES), jnp.bfloat16),
            jax.ShapeDtypeStruct((2 * width, 8 * LANES), jnp.bfloat16),
            jax.ShapeDtypeStruct((4, 8, LANES), jnp.float32),
        ),
        in_specs=[pl.BlockSpec(memory_space=pltpu.SMEM)] * 2
        + [pl.BlockSpec(memory_space=pltpu.VMEM)] * 2,
        out_specs=(pl.BlockSpec(memory_space=pltpu.VMEM),) * 3,
        compiler_params=pltpu.CompilerParams(vmem_limit_bytes=32 * 1024 * 1024),
        name="tables",
    )(start.reshape(1), material_table, material_table, spots)


def row_values(planes, row, height, sleepers, width):
    depth = planes.shape[1]
    parts = [planes[pl.ds(c * height + row, sleepers, stride=3 * height), :] for c in range(3)]
    material = planes[pl.ds(3 * sleepers * height + row, 1), :]
    number = lax.broadcasted_iota(jnp.int32, (width - 3 * sleepers, depth), 0)
    kind = jnp.where(number < 3 * NMAT, number % NMAT, -1).astype(jnp.float32)
    parts.append((kind == material).astype(jnp.float32))
    return jnp.concatenate(parts, axis=0)


def gather(spots, pieces, planes, sems):
    copies = []
    for n, (piece, first, count, plane, row, target) in enumerate(spots):
        src = pieces[piece]
        copies.append(
            pltpu.make_async_copy(
                src.at[plane : plane + count, row[0] : row[0] + row[1], :],
                planes.at[first : first + count, target : target + row[1], :],
                sems.at[n],
            )
        )
    for copy in copies:
        copy.start()
    for copy in copies:
        copy.wait()


def edge_kernel(sleepers, spots, *refs):
    *pieces, out, planes, sems = refs
    gather(spots, pieces, planes, sems)
    height, depth = planes.shape[1:]
    width = out.shape[2]
    spot = lax.broadcasted_iota(jnp.int32, (2 * HB, depth), 0)
    at = lax.broadcasted_iota(jnp.int32, (2 * HB, depth), 1)
    pick = (at == jnp.where(spot < HB, spot, spot + (depth - 2 * HB))).astype(jnp.bfloat16)
    flat = planes.reshape(planes.shape[0] * height, depth)

    def some_rows(block, carry):
        for line in range(8):
            row = 8 * block + line
            high, low = two_parts(row_values(flat, row, height, sleepers, width))
            out[row, :, :] = dot_t(pick, high) + dot_t(pick, low)
        return carry

    lax.fori_loop(0, height // 8, some_rows, 0)


def edges_of(spots, pieces, sleepers, height, depth):
    return pl.pallas_call(
        functools.partial(edge_kernel, sleepers, spots),
        out_shape=jax.ShapeDtypeStruct((height, 2 * HB, lanes_for(sleepers)), jnp.float32),
        in_specs=[pl.BlockSpec(memory_space=pl.ANY)] * len(pieces),
        out_specs=pl.BlockSpec(memory_space=pltpu.VMEM),
        scratch_shapes=[
            pltpu.VMEM((3 * sleepers + 1, height, depth), jnp.float32),
            pltpu.SemaphoreType.DMA((len(spots),)),
        ],
        compiler_params=pltpu.CompilerParams(vmem_limit_bytes=32 * 1024 * 1024),
        name="edge_columns",
    )(*pieces)


def field_kernel(sleepers, count, seglen, spots, scratch, *refs):
    pl.run_scoped(functools.partial(field_body, sleepers, count, seglen, spots, refs), *scratch)


def field_body(sleepers, count, seglen, spots, refs, *scratch):
    flags, left, right, tw, tc, vectors, edge, *pieces, out = refs
    (planes, sems, source, ghosts, coefs, made_source, made_coefs, lhs, lay,
     a1, a2, a3, wide, b1, b2, turn, pages, page_sems) = scratch
    height, depth = planes.shape[1:]
    flat = planes.reshape(planes.shape[0] * height, depth)
    ny = height - 2 * HB
    width = left.shape[2]
    chunks = width // LANES
    cells = 8 * seglen
    page_rows = pages.reshape(2 * count * 48, depth)
    lane = lax.broadcasted_iota(jnp.int32, (8, LANES), 1)
    sub = lax.broadcasted_iota(jnp.int32, (8, LANES), 0)

    def at(zm):
        return pl.ds(8 * (zm + 1), 8)

    def around(first, last):
        before = pltpu.roll(last, 1, 0)
        after = pltpu.roll(first, 7, 0)
        return (
            jnp.where(sub == 0, pltpu.roll(before, HALF, 1), before),
            jnp.where(sub == 7, pltpu.roll(after, HALF, 1), after),
        )

    def line_at(row, zm):
        return pl.ds(pl.multiple_of((row & 15) * cells, 8) + 8 * zm, 8)

    def column(q):
        part, c = divmod(q, 3)
        return slice((2 * c + part) * LANES, (2 * c + part + 1) * LANES)

    def read_source(row, q, zm):
        if zm == -1:
            return ghosts[row & 15, q, :8, :]
        if zm == seglen:
            return ghosts[row & 15, q, 8:, :]
        return source[line_at(row, zm), column(q)]

    def reader(ring):
        def read(row, q, zm):
            outside = ((row < HY) & (flags[0] == 1)) | ((row >= HY + ny) & (flags[1] == 1))
            return ring[jnp.where(outside, 4, row & 3), q, at(zm), :]

        return read

    def produce(pair):
        def lay_out(k):
            srow = jnp.clip(2 * pair - 2 + k + (HB - HY), 0, height - 1)
            values = row_values(flat, srow, height, sleepers, width)
            for n in range(chunks):
                span = slice(n * LANES, (n + 1) * LANES)
                lay[k * chunks + n, HB : HB + depth, :] = jnp.transpose(values[span])
                lay[k * chunks + n, :HB, :] = left[srow, :, span]
                lay[k * chunks + n, HB + depth :, :] = right[srow, :, span]

        def split():
            halves = [[], []]
            for k in range(2):
                for half in range(2):
                    for zm in range(seglen):
                        spot = pl.ds(half * cells + zm, 8, stride=seglen)
                        pieces_at = [lay[k * chunks + n, spot, :] for n in range(chunks)]
                        halves[half].append(jnp.concatenate(pieces_at, axis=1))
            values = jnp.concatenate(
                [jnp.concatenate(half, axis=0) for half in halves], axis=1
            )
            high, low = two_parts(values)
            lhs[:, : 2 * width] = high
            lhs[:, 2 * width : 4 * width] = low
            lhs[:, 4 * width :] = high

        def spectrum(c):
            span = slice(2 * c * LANES, 2 * (c + 1) * LANES)
            made_source[:, span] = dot(lhs[...], tw[:, span])

        def fields(f):
            span = slice(f * LANES, (f + 2) * LANES)
            made_coefs[:, span] = dot(lhs[:, : 2 * width], tc[:, span])

        return [
            functools.partial(lay_out, 0),
            functools.partial(lay_out, 1),
            split,
            *[functools.partial(spectrum, c) for c in range(3)],
            *[functools.partial(fields, f) for f in range(0, 8, 2)],
        ]

    def commit(pair):
        for k in range(2):
            row = 2 * pair - 2 + k
            for zm in range(seglen):
                rows = slice(k * cells + 8 * zm, k * cells + 8 * zm + 8)
                for n in range(6):
                    span = slice(n * LANES, (n + 1) * LANES)
                    source[line_at(row, zm), span] = made_source[rows, span]
                for n in range(7):
                    span = slice(n * LANES, (n + 1) * LANES)
                    coefs[line_at(row, zm), span] = made_coefs[rows, span]
            for q in range(6):
                first = made_source[k * cells : k * cells + 8, column(q)]
                last = made_source[(k + 1) * cells - 8 : (k + 1) * cells, column(q)]
                ghosts[row & 15, q, :8, :], ghosts[row & 15, q, 8:, :] = around(first, last)

    def apply(src, row, emit, shift=None, extra=None):
        prev = [[src(row + k, q, -1) for q in range(6)] for k in range(2)]
        cur = [[src(row + k, q, 0) for q in range(6)] for k in range(2)]
        held = None
        for zm in range(seglen):
            nxt = [None, None]
            for k in range(2):
                nxt[k] = [src(row + k, q, zm + 1) for q in range(6)]
                outer = [src(row + 3 * k - 1, q, zm) for q in range(6)]
                f = [
                    coefs[line_at(row + k, zm), n * LANES : (n + 1) * LANES] for n in range(7)
                ]
                if extra is not None:
                    added = [extra[0](row + k, q, zm) for q in range(6)]
                if held is not None:
                    emit(*held)
                diagonal = f[:3]
                if shift is not None:
                    diagonal = [d + shift for d in diagonal]
                matrix = (
                    (diagonal[0], f[3], f[4]),
                    (f[3], diagonal[1], f[5]),
                    (f[4], f[5], diagonal[2]),
                )
                results = []
                for q in range(6):
                    part, c = divmod(q, 3)
                    near = (outer[q] + cur[1 - k][q]) + (prev[k][q] + nxt[k][q])
                    mine = cur[k][3 * part : 3 * part + 3]
                    own = matrix[c][0] * mine[0] + matrix[c][1] * mine[1] + matrix[c][2] * mine[2]
                    damp = f[6] * cur[k][3 * (1 - part) + c]
                    total = near + own
                    total = total + damp if part == 0 else total - damp
                    if extra is not None:
                        total = total + extra[1] * added[q]
                    results.append(total)
                held = (k, zm, results)
            prev, cur = cur, nxt
        emit(*held)

    def stage(src, dst, row, extra=None, between=None):
        ends = {}

        def emit(k, zm, results):
            if zm == HB - 1:
                results = [value * edge[0] for value in results]
            if zm == (HB + depth) % seglen:
                results = [value * edge[1] for value in results]
            slot = (row + k) & 3
            for q in range(6):
                dst[slot, q, at(zm), :] = results[q]
            if zm in (0, seglen - 1):
                ends[k, zm] = results
            if zm == seglen - 1:
                for q in range(6):
                    dst[slot, q, at(-1), :], dst[slot, q, at(seglen), :] = around(
                        ends[k, 0][q], results[q]
                    )
            if between is not None and k == 1:
                between()

        apply(src, row, emit, extra=extra)

    def last_stage(row):
        def emit(k, zm, results):
            for c in range(3):
                real, imag = results[c], results[3 + c]
                first = jnp.where(lane < HALF, real, pltpu.roll(imag, HALF, 1))
                second = jnp.where(lane < HALF, pltpu.roll(real, HALF, 1), imag)
                turn[3 * k + c, pl.ds(zm, 8, stride=seglen), :] = first
                turn[3 * k + c, pl.ds(cells + zm, 8, stride=seglen), :] = second

        apply(reader(b2), row, emit, shift=vectors[3])

    stages = (
        lambda base, more: stage(read_source, a1, base - 1, None, more),
        lambda base, more: stage(reader(a1), a2, base - 2, (read_source, vectors[0]), more),
        lambda base, more: stage(reader(a2), a3, base - 3, None, more),
        lambda base, more: stage(reader(a3), wide, base - 4, (read_source, vectors[1]), more),
        lambda base, more: stage(reader(wide), b1, base - 5, None, more),
        lambda base, more: stage(reader(b1), b2, base - 6, (reader(wide), vectors[2]), more),
    )

    def finish(pair):
        done = pair - HB
        block = done >> 2
        start = pl.multiple_of((block & 1) * (count * 48), 8) + 2 * (done & 3)

        def page(k, c):
            turned = jnp.transpose(turn[3 * k + c, HB : HB + depth, :])
            for part in range(2):
                rows = pl.ds(start + (part * 3 + c) * 8 + k, count, stride=48)
                page_rows[rows, :] = turned[part * HALF : part * HALF + count]

        return [functools.partial(page, k, c) for k in range(2) for c in range(3)]

    def page_copy(block):
        return pltpu.make_async_copy(
            pages.at[block & 1],
            out.at[:, :, :, pl.ds(pl.multiple_of(8 * block, 8), 8), :],
            page_sems.at[block & 1],
        )

    def ramp(pair, carry):
        base = 2 * pair - 2
        commit(pair)
        for step in produce(pair + 1):
            step()
        for t, run in enumerate(stages):

            @pl.when(base >= 2 * t + 2)
            def _():
                run(base, None)

        @pl.when(base >= 14)
        def _():
            last_stage(base - 7)

        return carry

    def steady(pair, carry):
        base = 2 * pair - 2
        done = pair - 1 - HB

        @pl.when(((done & 3) == 0) & (done >= 8))
        def _():
            page_copy((done >> 2) - 2).wait()

        commit(pair)
        pending = []
        making, turning = produce(pair + 1), finish(pair - 1)
        while making or turning:
            if turning:
                pending.append(turning.pop(0))
            if making:
                pending.append(making.pop(0))
        slots = 6 * seglen
        count_of = len(pending)
        seen = [0]

        def between():
            seen[0] += 1
            while pending and (count_of - len(pending)) * slots < seen[0] * count_of:
                pending.pop(0)()

        for run in stages:
            run(base, between)
        while pending:
            pending.pop(0)()
        last_stage(base - 7)

        @pl.when((done & 3) == 3)
        def _():
            page_copy(done >> 2).start()

        return carry

    gather(spots, pieces, planes, sems)
    for ring in (a1, a2, a3, wide, b1, b2):
        for q in range(6):
            ring[4, q, :, :] = jnp.zeros(ring.shape[2:], jnp.float32)
    for step in produce(0):
        step()
    final = HB + ny // 2 - 1
    lax.fori_loop(0, HB + 1, ramp, 0)
    lax.fori_loop(HB + 1, final + 1, steady, 0)
    for step in finish(final):
        step()
    blocks = ny // 8
    page_copy(blocks - 1).start()
    for block in range(max(blocks - 2, 0), blocks):
        page_copy(block).wait()


def solve_field(spots, pieces, flags, left, right, tw, tc, vectors, edge, sleepers, count):
    height, _, width = left.shape
    depth = pieces[0].shape[2]
    ny = height - 2 * HB
    seglen = (depth + 2 * HB) // SEGS
    cells = 8 * seglen
    chunks = width // LANES
    ring = pltpu.VMEM((5, 6, 8 * (seglen + 2), LANES), jnp.float32)
    whole = pl.BlockSpec(memory_space=pltpu.VMEM)
    scratch = (
        pltpu.VMEM((3 * sleepers + 1, height, depth), jnp.float32),
        pltpu.SemaphoreType.DMA((len(spots),)),
        pltpu.VMEM((16 * cells, 6 * LANES), jnp.float32),
        pltpu.VMEM((16, 6, 16, LANES), jnp.float32),
        pltpu.VMEM((16 * cells, 7 * LANES), jnp.float32),
        pltpu.VMEM((2 * cells, 6 * LANES), jnp.float32),
        pltpu.VMEM((2 * cells, 8 * LANES), jnp.float32),
        pltpu.VMEM((2 * cells, 6 * width), jnp.bfloat16),
        pltpu.VMEM((2 * chunks, 2 * cells, LANES), jnp.float32),
        ring, ring, ring, ring, ring, ring,
        pltpu.VMEM((6, 2 * cells, LANES), jnp.float32),
        pltpu.VMEM((2, count, 2, 3, 8, depth), jnp.float32),
        pltpu.SemaphoreType.DMA((2,)),
    )
    return pl.pallas_call(
        functools.partial(field_kernel, sleepers, count, seglen, spots, scratch),
        out_shape=jax.ShapeDtypeStruct((count, 2, 3, ny, depth), jnp.float32),
        in_specs=[pl.BlockSpec(memory_space=pltpu.SMEM)]
        + [whole] * 6
        + [pl.BlockSpec(memory_space=pl.ANY)] * len(pieces),
        out_specs=pl.BlockSpec(memory_space=pl.ANY),
        compiler_params=pltpu.CompilerParams(vmem_limit_bytes=40 * 1024 * 1024),
        name="adjoint_field",
    )(flags, left, right, tw, tc, vectors, edge, *pieces)


def local(loads, sleeper_pos, material, material_table):
    ka = lax.axis_size("ka")
    gy, gz = lax.axis_size("gy"), lax.axis_size("gz")
    count = KW // ka
    wave_start = lax.axis_index("ka") * count
    sleepers = ka * loads.shape[0]
    own = 3 * loads.shape[0]
    ny, depth = material.shape
    height = ny + 2 * HB
    loads = loads.reshape(own, ny, depth)
    material = material.astype(jnp.float32)[None]

    def shift(array, axis, size, by):
        pairs = [(i, i + by) for i in range(size) if 0 <= i + by < size]
        return lax.ppermute(array, axis, pairs)

    turns = [[(i, (i + step) % ka) for i in range(ka)] for step in range(1, ka)]
    ends = jnp.concatenate([loads[:, :HB], loads[:, ny - HB :]], axis=1)
    got_ends = [lax.ppermute(ends, "ka", turn) for turn in turns]
    inner = loads[:, HB : ny - HB]
    got_inner = [lax.ppermute(inner, "ka", turn) for turn in turns]
    all_pos = [sleeper_pos] + [lax.ppermute(sleeper_pos, "ka", turn) for turn in turns]
    tw, tc, vectors = tables(
        jnp.concatenate(all_pos), material_table, wave_start, count, lanes_for(sleepers)
    )
    tw, tc, vectors, tied = lax.optimization_barrier((tw, tc, vectors, loads))
    low = jnp.concatenate([tied[:, :HB], material[:, :HB]], axis=0)
    high = jnp.concatenate([tied[:, ny - HB :], material[:, ny - HB :]], axis=0)
    above, below = shift(high, "gy", gy, 1), shift(low, "gy", gy, -1)

    pieces = [loads, material, above, below]
    spots = [
        (0, 0, own, 0, (0, ny), HB),
        (1, 3 * sleepers, 1, 0, (0, ny), HB),
        (2, 0, own, 0, (0, HB), 0),
        (2, 3 * sleepers, 1, own, (0, HB), 0),
        (3, 0, own, 0, (0, HB), HB + ny),
        (3, 3 * sleepers, 1, own, (0, HB), HB + ny),
    ]
    for step, (outer, middle) in enumerate(zip(got_ends, got_inner)):
        first = own * (step + 1)
        number = len(pieces)
        pieces += [
            outer,
            middle,
            shift(outer[:, HB:], "gy", gy, 1),
            shift(outer[:, :HB], "gy", gy, -1),
        ]
        spots += [
            (number, first, own, 0, (0, HB), HB),
            (number, first, own, 0, (HB, HB), ny),
            (number + 1, first, own, 0, (0, ny - 2 * HB), 2 * HB),
            (number + 2, first, own, 0, (0, HB), 0),
            (number + 3, first, own, 0, (0, HB), HB + ny),
        ]

    y_at, z_at = lax.axis_index("gy"), lax.axis_index("gz")
    flags = jnp.stack([y_at == 0, y_at == gy - 1]).astype(jnp.int32)
    sub = jnp.arange(8)[:, None]
    lane = jnp.arange(LANES)[None, :]
    edge = jnp.stack(
        [
            jnp.where((z_at == 0) & (sub == 0) & (lane < HALF), 0.0, 1.0),
            jnp.where((z_at == gz - 1) & (sub == 7) & (lane >= HALF), 0.0, 1.0),
        ]
    ).astype(jnp.float32)
    pieces[-1], flags, edge = lax.optimization_barrier((pieces[-1], flags, edge))

    columns = edges_of(spots, pieces, sleepers, height, depth)
    left = shift(columns[:, HB:], "gz", gz, 1)
    right = shift(columns[:, :HB], "gz", gz, -1)
    return solve_field(
        spots, pieces, flags, left, right, tw, tc, vectors, edge, sleepers, count
    )


def solution(mesh):
    return jax.shard_map(
        local,
        mesh=mesh,
        in_specs=(P("ka", None, "gy", "gz"), P("ka"), P("gy", "gz"), P()),
        out_specs=P("ka", None, None, "gy", "gz"),
        check_vma=False,
    )
```

profile of v0, /device:TPU:1, one launch (start us, length us, event | category | flops | bytes accessed | tf_op | source)
XLA Modules:
  0.0 98.2 jit_solution(10292748966098257512)
XLA Ops:
  0.0 2.0 %collective-permute-start.2 = (s32[16]{0:T(128)}, s32[16]{0:T(128)S(1)}, u32[]{:S(2)}, u32[]{:S(2)}) collective-permute-start(s32[16]{0:T(128)} %param.5), channel_id=1, source_target_pairs={{0,16},{16,0},{1,17},{17,1},{2,18},{18,2},{3,19},{19,3},{4,20},{20... | collective-permute-start | bytes 200 | tf_op jit(solution)/shard_map/ppermute | solution.py:519
  2.0 1.1 %fusion.1 = (f32[48,8,128]{2,1,0:T(8,128)S(1)}, f32[48,8,128]{2,1,0:T(8,128)S(1)}) fusion(f32[48,32,128]{2,1,0:T(8,128)} %bitcast.6), kind=kLoop, calls=%fused_computation.14 | loop fusion | bytes 786432 | tf_op jit(solution)/shard_map/slice | solution.py:515
  3.1 0.1 collective-permute-start
  3.3 1.0 %slice.49 = f32[48,16,128]{2,1,0:T(8,128)S(1)} slice(f32[48,32,128]{2,1,0:T(8,128)} %bitcast.7), slice={[0:48], [8:24], [0:128]} | slice | bytes 786432 | tf_op jit(solution)/shard_map/slice | solution.py:517
  4.3 1.5 %collective-permute-start.5 = (f32[48,16,128]{2,1,0:T(8,128)S(1)}, f32[48,16,128]{2,1,0:T(8,128)S(1)}, u32[]{:S(2)}, u32[]{:S(2)}) collective-permute-start(f32[48,16,128]{2,1,0:T(8,128)S(1)} %slice.49), channel_id=1, source_target_pairs={{0,16},{16,0},{1,17},{17,1},{2,18},{18,2},{3,19},{19,3},{4,20},{20... | collective-permute-start | bytes 1179656 | tf_op jit(solution)/shard_map/ppermute | solution.py:518
  5.8 0.7 convert_bitcast_fusion.refs_1_.refs_8_
  6.5 0.1 and_select_fusion
  6.6 0.0 collective-permute-done.2
  6.6 0.7 pad_add_fusion
  7.3 0.1 broadcast_in_dim.24.positions
  7.4 0.7 copy-done.2
  8.1 0.9 tables.1
  9.0 1.1 %fusion = (f32[48,8,128]{2,1,0:T(8,128)S(1)}, f32[48,8,128]{2,1,0:T(8,128)S(1)}) fusion(f32[48,32,128]{2,1,0:T(8,128)} %bitcast.8), kind=kLoop, calls=%fused_computation.13 | loop fusion | bytes 786432 | tf_op jit(solution)/shard_map/slice | solution.py:524
  10.1 3.2 %collective-permute-start.3 = (f32[49,8,128]{2,1,0:T(8,128)S(1)}, f32[49,8,128]{2,1,0:T(8,128)S(1)}, u32[]{:S(2)}, u32[]{:S(2)}) collective-permute-start(f32[49,8,128]{2,1,0:T(8,128)S(1)} %pad_maximum_fusion.1), channel_id=1, source_target_pairs={{0,4},{4,8},{8,12},{1,5},{5,9},{9,13},{2,6},{6,10},{10,14},{3,7},{... | collective-permute-start | bytes 602120 | tf_op jit(solution)/shard_map/ppermute | solution.py:512
  13.3 1.3 %collective-permute-start.4 = (f32[49,8,128]{2,1,0:T(8,128)S(1)}, f32[49,8,128]{2,1,0:T(8,128)S(1)}, u32[]{:S(2)}, u32[]{:S(2)}) collective-permute-start(f32[49,8,128]{2,1,0:T(8,128)S(1)} %pad_maximum_fusion.2), channel_id=1, source_target_pairs={{4,0},{8,4},{12,8},{5,1},{9,5},{13,9},{6,2},{10,6},{14,10},{7,3},{... | collective-permute-start | bytes 602120 | tf_op jit(solution)/shard_map/ppermute | solution.py:512
  14.6 0.0 collective-permute-done.refs_4_.refs_11_
  14.6 4.0 %collective-permute-start.6 = (f32[48,8,128]{2,1,0:T(8,128)S(1)}, f32[48,8,128]{2,1,0:T(8,128)S(1)}, u32[]{:S(2)}, u32[]{:S(2)}) collective-permute-start(f32[48,8,128]{2,1,0:T(8,128)S(1)} %get-tuple-element.31), channel_id=1, source_target_pairs={{0,4},{4,8},{8,12},{1,5},{5,9},{9,13},{2,6},{6,10},{10,14},{3,7},{... | collective-permute-start | bytes 589832 | tf_op jit(solution)/shard_map/ppermute | solution.py:512
  18.7 1.3 %collective-permute-start.1 = (f32[48,8,128]{2,1,0:T(8,128)S(1)}, f32[48,8,128]{2,1,0:T(8,128)S(1)}, u32[]{:S(2)}, u32[]{:S(2)}) collective-permute-start(f32[48,8,128]{2,1,0:T(8,128)S(1)} %get-tuple-element.32), channel_id=1, source_target_pairs={{4,0},{8,4},{12,8},{5,1},{9,5},{13,9},{6,2},{10,6},{14,10},{7,3},{... | collective-permute-start | bytes 589832 | tf_op jit(solution)/shard_map/ppermute | solution.py:512
  20.0 0.1 add_convert_fusion.refs_0_
  20.0 5.0 %collective-permute-done.1.refs_7_.refs_14_ = f32[48,8,128]{2,1,0:T(8,128)S(1)} collective-permute-done((f32[48,8,128]{2,1,0:T(8,128)S(1)}, f32[48,8,128]{2,1,0:T(8,128)S(1)}, u32[]{:S(2)}, u32[]{:S(2)}) %collective-permute-start.1) | collective-permute-done | bytes 196640 | tf_op jit(solution)/shard_map/ppermute | solution.py:512
  25.1 0.0 collective-permute-done.3.refs_2_.refs_9_
  25.1 0.0 collective-permute-done.4.refs_3_.refs_10_
  25.1 0.0 collective-permute-done.5.refs_5_.refs_12_
  25.1 0.0 collective-permute-done.6.refs_6_.refs_13_
  25.1 0.0 copy-start
  25.1 1.1 %copy-done = f32[16,3,32,128]{3,2,1,0:T(8,128)S(1)} copy-done((f32[16,3,32,128]{3,2,1,0:T(8,128)S(1)}, f32[16,3,32,128]{3,2,1,0:T(8,128)}, u32[]{:S(2)}) %copy-start) | copy-done | bytes 786456
  26.2 2.7 %edge_columns.1 = f32[48,16,128]{2,1,0:T(8,128)S(1)} custom-call(f32[48,32,128]{2,1,0:T(8,128)S(1)} %bitcast.9, f32[1,32,128]{2,1,0:T(8,128)S(1)} %convert_bitcast_fusion.refs_1_.refs_8_, f32[49,8,128]{2,1,0:T(8,128)S(1)} %collective-permute-done.3.refs_2_.refs_9_, f32[49,8,128]{2,1,0:T(8,128)S(1)} %collective-permute-done.4.refs_3_.refs_10_, ...), custom_call_target="tpu_custom_call" | custom-call | tf_op jit(solution)/shard_map/edge_columns/pallas_call | solution.py:166
  29.0 5.4 %collective-permute-start.8 = (f32[48,8,128]{2,1,0:T(8,128)S(1)}, f32[48,8,128]{2,1,0:T(8,128)S(1)}, u32[]{:S(2)}, u32[]{:S(2)}) collective-permute-start(f32[48,8,128]{2,1,0:T(8,128)S(1)} %get-tuple-element.29), channel_id=1, source_target_pairs={{1,0},{2,1},{3,2},{5,4},{6,5},{7,6},{9,8},{10,9},{11,10},{13,12},{... | collective-permute-start | bytes 589832 | tf_op jit(solution)/shard_map/ppermute | solution.py:512
  34.4 3.0 %collective-permute-start.7 = (f32[48,8,128]{2,1,0:T(8,128)S(1)}, f32[48,8,128]{2,1,0:T(8,128)S(1)}, u32[]{:S(2)}, u32[]{:S(2)}) collective-permute-start(f32[48,8,128]{2,1,0:T(8,128)S(1)} %get-tuple-element.30), channel_id=1, source_target_pairs={{0,1},{1,2},{2,3},{4,5},{5,6},{6,7},{8,9},{9,10},{10,11},{12,13},{... | collective-permute-start | bytes 589832 | tf_op jit(solution)/shard_map/ppermute | solution.py:512
  37.5 1.4 %collective-permute-done.8.refs_2_ = f32[48,8,128]{2,1,0:T(8,128)S(1)} collective-permute-done((f32[48,8,128]{2,1,0:T(8,128)S(1)}, f32[48,8,128]{2,1,0:T(8,128)S(1)}, u32[]{:S(2)}, u32[]{:S(2)}) %collective-permute-start.8) | collective-permute-done | bytes 196640 | tf_op jit(solution)/shard_map/ppermute | solution.py:512
  38.9 1.2 %collective-permute-done.7.refs_1_ = f32[48,8,128]{2,1,0:T(8,128)S(1)} collective-permute-done((f32[48,8,128]{2,1,0:T(8,128)S(1)}, f32[48,8,128]{2,1,0:T(8,128)S(1)}, u32[]{:S(2)}, u32[]{:S(2)}) %collective-permute-start.7) | collective-permute-done | bytes 196640 | tf_op jit(solution)/shard_map/ppermute | solution.py:512
  40.0 58.2 %adjoint_field.1 = f32[64,2,3,32,128]{4,3,2,1,0:T(8,128)} custom-call(s32[2]{0:T(128)S(1)} %add_convert_fusion.refs_0_, f32[48,8,128]{2,1,0:T(8,128)S(1)} %collective-permute-done.7.refs_1_, f32[48,8,128]{2,1,0:T(8,128)S(1)} %collective-permute-done.8.refs_2_, bf16[768,768]{1,0:T(8,128)(2,1)S(1)} %get-tuple-element.21.refs_3_, ...), custom_call_target="tpu_custom_call" | custom-call | tf_op jit(solution)/shard_map/adjoint_field/pallas_call | solution.py:486
  (14 shorter events, 0.2 us)
Async XLA Ops:
  0.0 40.0 %copy-start.1 = (f32[16,3,32,128]{3,2,1,0:T(8,128)S(1)}, f32[16,3,32,128]{3,2,1,0:T(8,128)}, u32[]{:S(2)}) copy-start(f32[16,3,32,128]{3,2,1,0:T(8,128)} %param.4) | copy-start | bytes 2359300
  0.0 6.6 %collective-permute-start.2 = (s32[16]{0:T(128)}, s32[16]{0:T(128)S(1)}, u32[]{:S(2)}, u32[]{:S(2)}) collective-permute-start(s32[16]{0:T(128)} %param.5), channel_id=1, source_target_pairs={{0,16},{16,0},{1,17},{17,1},{2,18},{18,2},{3,19},{19,3},{4,20},{20... | collective-permute-start | bytes 200 | tf_op jit(solution)/shard_map/ppermute | solution.py:519
  3.1 11.5 %collective-permute-start = (f32[48,16,128]{2,1,0:T(8,128)S(1)}, f32[48,16,128]{2,1,0:T(8,128)S(1)}, u32[]{:S(2)}, u32[]{:S(2)}) collective-permute-start(f32[48,16,128]{2,1,0:T(8,128)S(1)} %pad_maximum_fusion), channel_id=1, source_target_pairs={{0,16},{16,0},{1,17},{17,1},{2,18},{18,2},{3,19},{19,3},{4,20},{20... | collective-permute-start | bytes 1179656 | tf_op jit(solution)/shard_map/ppermute | solution.py:516
  4.3 20.8 %collective-permute-start.5 = (f32[48,16,128]{2,1,0:T(8,128)S(1)}, f32[48,16,128]{2,1,0:T(8,128)S(1)}, u32[]{:S(2)}, u32[]{:S(2)}) collective-permute-start(f32[48,16,128]{2,1,0:T(8,128)S(1)} %slice.49), channel_id=1, source_target_pairs={{0,16},{16,0},{1,17},{17,1},{2,18},{18,2},{3,19},{19,3},{4,20},{20... | collective-permute-start | bytes 1179656 | tf_op jit(solution)/shard_map/ppermute | solution.py:518
  7.4 0.7 copy-start.2
  10.1 15.0 %collective-permute-start.3 = (f32[49,8,128]{2,1,0:T(8,128)S(1)}, f32[49,8,128]{2,1,0:T(8,128)S(1)}, u32[]{:S(2)}, u32[]{:S(2)}) collective-permute-start(f32[49,8,128]{2,1,0:T(8,128)S(1)} %pad_maximum_fusion.1), channel_id=1, source_target_pairs={{0,4},{4,8},{8,12},{1,5},{5,9},{9,13},{2,6},{6,10},{10,14},{3,7},{... | collective-permute-start | bytes 602120 | tf_op jit(solution)/shard_map/ppermute | solution.py:512
  13.3 11.8 %collective-permute-start.4 = (f32[49,8,128]{2,1,0:T(8,128)S(1)}, f32[49,8,128]{2,1,0:T(8,128)S(1)}, u32[]{:S(2)}, u32[]{:S(2)}) collective-permute-start(f32[49,8,128]{2,1,0:T(8,128)S(1)} %pad_maximum_fusion.2), channel_id=1, source_target_pairs={{4,0},{8,4},{12,8},{5,1},{9,5},{13,9},{6,2},{10,6},{14,10},{7,3},{... | collective-permute-start | bytes 602120 | tf_op jit(solution)/shard_map/ppermute | solution.py:512
  14.6 10.4 %collective-permute-start.6 = (f32[48,8,128]{2,1,0:T(8,128)S(1)}, f32[48,8,128]{2,1,0:T(8,128)S(1)}, u32[]{:S(2)}, u32[]{:S(2)}) collective-permute-start(f32[48,8,128]{2,1,0:T(8,128)S(1)} %get-tuple-element.31), channel_id=1, source_target_pairs={{0,4},{4,8},{8,12},{1,5},{5,9},{9,13},{2,6},{6,10},{10,14},{3,7},{... | collective-permute-start | bytes 589832 | tf_op jit(solution)/shard_map/ppermute | solution.py:512
  18.7 6.4 %collective-permute-start.1 = (f32[48,8,128]{2,1,0:T(8,128)S(1)}, f32[48,8,128]{2,1,0:T(8,128)S(1)}, u32[]{:S(2)}, u32[]{:S(2)}) collective-permute-start(f32[48,8,128]{2,1,0:T(8,128)S(1)} %get-tuple-element.32), channel_id=1, source_target_pairs={{4,0},{8,4},{12,8},{5,1},{9,5},{13,9},{6,2},{10,6},{14,10},{7,3},{... | collective-permute-start | bytes 589832 | tf_op jit(solution)/shard_map/ppermute | solution.py:512
  25.1 1.1 %copy-start = (f32[16,3,32,128]{3,2,1,0:T(8,128)S(1)}, f32[16,3,32,128]{3,2,1,0:T(8,128)}, u32[]{:S(2)}) copy-start(f32[16,3,32,128]{3,2,1,0:T(8,128)} %param.4) | copy-start | bytes 2359300
  29.0 9.9 %collective-permute-start.8 = (f32[48,8,128]{2,1,0:T(8,128)S(1)}, f32[48,8,128]{2,1,0:T(8,128)S(1)}, u32[]{:S(2)}, u32[]{:S(2)}) collective-permute-start(f32[48,8,128]{2,1,0:T(8,128)S(1)} %get-tuple-element.29), channel_id=1, source_target_pairs={{1,0},{2,1},{3,2},{5,4},{6,5},{7,6},{9,8},{10,9},{11,10},{13,12},{... | collective-permute-start | bytes 589832 | tf_op jit(solution)/shard_map/ppermute | solution.py:512
  34.4 5.6 %collective-permute-start.7 = (f32[48,8,128]{2,1,0:T(8,128)S(1)}, f32[48,8,128]{2,1,0:T(8,128)S(1)}, u32[]{:S(2)}, u32[]{:S(2)}) collective-permute-start(f32[48,8,128]{2,1,0:T(8,128)S(1)} %get-tuple-element.30), channel_id=1, source_target_pairs={{0,1},{1,2},{2,3},{4,5},{5,6},{6,7},{8,9},{9,10},{10,11},{12,13},{... | collective-permute-start | bytes 589832 | tf_op jit(solution)/shard_map/ppermute | solution.py:512
where the time goes:
time: 98.7 us; the launch traced here: 98.2 us
  Pallas kernels  61.8 us (63%)
  starting transfers between devices  21.9 us (22%)
  waiting for transfers between devices  7.64 us (8%)
  local copies, waits for them, and re-layouts  5.08 us (5%)
  other arithmetic  1.7 us (2%)
    pallas_call x1, Pallas kernels, solve_field(): pl.pallas_call(functools.partial(field_kernel, sleepers, count, seglen, s...  58.2 us
    ppermute x6, starting transfers between devices, shift(): return lax.ppermute(array, axis, pairs)  18.3 us
    ppermute x6, waiting for transfers between devices, shift(): return lax.ppermute(array, axis, pairs)  7.63 us
    pallas_call x1, Pallas kernels, edges_of(): pl.pallas_call(functools.partial(edge_kernel, sleepers, spots), out_shape...  2.7 us
    ppermute x1, starting transfers between devices, local(): lax.ppermute(sleeper_pos, 'ka', turn)  2.04 us
  transfers between devices with their start and end apart: 9, of which 3 were waited for; matrix products, arithmetic and copies ran while one was open for 5% of the time, Pallas kernels for 1%

commit v1 on v0

--- a/solution.py
+++ b/solution.py
@@ -166,7 +166,8 @@
     return pl.pallas_call(
         functools.partial(edge_kernel, sleepers, spots),
         out_shape=jax.ShapeDtypeStruct((height, 2 * HB, lanes_for(sleepers)), jnp.float32),
-        in_specs=[pl.BlockSpec(memory_space=pl.ANY)] * len(pieces),
+        in_specs=[pl.BlockSpec(memory_space=pltpu.HBM)]
+        + [pl.BlockSpec(memory_space=pl.ANY)] * (len(pieces) - 1),
         out_specs=pl.BlockSpec(memory_space=pltpu.VMEM),
         scratch_shapes=[
             pltpu.VMEM((3 * sleepers + 1, height, depth), jnp.float32),
@@ -286,21 +287,14 @@
                 ghosts[row & 15, q, :8, :], ghosts[row & 15, q, 8:, :] = around(first, last)
 
     def apply(src, row, emit, shift=None, extra=None):
-        prev = [[src(row + k, q, -1) for q in range(6)] for k in range(2)]
-        cur = [[src(row + k, q, 0) for q in range(6)] for k in range(2)]
-        held = None
-        for zm in range(seglen):
-            nxt = [None, None]
-            for k in range(2):
-                nxt[k] = [src(row + k, q, zm + 1) for q in range(6)]
-                outer = [src(row + 3 * k - 1, q, zm) for q in range(6)]
+        for k in range(2):
+            prev = [src(row + k, q, -1) for q in range(6)]
+            cur = [src(row + k, q, 0) for q in range(6)]
+            for zm in range(seglen):
+                nxt = [src(row + k, q, zm + 1) for q in range(6)]
                 f = [
                     coefs[line_at(row + k, zm), n * LANES : (n + 1) * LANES] for n in range(7)
                 ]
-                if extra is not None:
-                    added = [extra[0](row + k, q, zm) for q in range(6)]
-                if held is not None:
-                    emit(*held)
                 diagonal = f[:3]
                 if shift is not None:
                     diagonal = [d + shift for d in diagonal]
@@ -312,18 +306,18 @@
                 results = []
                 for q in range(6):
                     part, c = divmod(q, 3)
-                    near = (outer[q] + cur[1 - k][q]) + (prev[k][q] + nxt[k][q])
-                    mine = cur[k][3 * part : 3 * part + 3]
+                    near = src(row + k - 1, q, zm) + src(row + k + 1, q, zm)
+                    near = near + (prev[q] + nxt[q])
+                    mine = cur[3 * part : 3 * part + 3]
                     own = matrix[c][0] * mine[0] + matrix[c][1] * mine[1] + matrix[c][2] * mine[2]
-                    damp = f[6] * cur[k][3 * (1 - part) + c]
+                    damp = f[6] * cur[3 * (1 - part) + c]
                     total = near + own
                     total = total + damp if part == 0 else total - damp
                     if extra is not None:
-                        total = total + extra[1] * added[q]
+                        total = total + extra[1] * extra[0](row + k, q, zm)
                     results.append(total)
-                held = (k, zm, results)
-            prev, cur = cur, nxt
-        emit(*held)
+                emit(k, zm, results)
+                prev, cur = cur, nxt
 
     def stage(src, dst, row, extra=None, between=None):
         ends = {}
@@ -343,7 +337,7 @@
                     dst[slot, q, at(-1), :], dst[slot, q, at(seglen), :] = around(
                         ends[k, 0][q], results[q]
                     )
-            if between is not None and k == 1:
+            if between is not None:
                 between()
 
         apply(src, row, emit, extra=extra)
@@ -421,7 +415,7 @@
                 pending.append(turning.pop(0))
             if making:
                 pending.append(making.pop(0))
-        slots = 6 * seglen
+        slots = 12 * seglen
         count_of = len(pending)
         seen = [0]
 
@@ -488,7 +482,8 @@
         out_shape=jax.ShapeDtypeStruct((count, 2, 3, ny, depth), jnp.float32),
         in_specs=[pl.BlockSpec(memory_space=pltpu.SMEM)]
         + [whole] * 6
-        + [pl.BlockSpec(memory_space=pl.ANY)] * len(pieces),
+        + [pl.BlockSpec(memory_space=pltpu.HBM)]
+        + [pl.BlockSpec(memory_space=pl.ANY)] * (len(pieces) - 1),
         out_specs=pl.BlockSpec(memory_space=pl.ANY),
         compiler_params=pltpu.CompilerParams(vmem_limit_bytes=40 * 1024 * 1024),
         name="adjoint_field",

time: 98.7 us -> 97.2 us (0.985)
  Pallas kernels: 61.8 us -> 60.2 us
    pallas_call x1, Pallas kernels: 58.2 us -> 56.7 us  [solve_field(): pl.pallas_call(functools.partial(field_kernel, sleepers, count, seglen, s...]
where the time goes in v1:
time: 97.2 us; the launch traced here: 96.7 us
  Pallas kernels  60.2 us (62%)
  starting transfers between devices  21.9 us (23%)
  waiting for transfers between devices  7.64 us (8%)
  local copies, waits for them, and re-layouts  5.08 us (5%)
  other arithmetic  1.7 us (2%)
    pallas_call x1, Pallas kernels, solve_field(): pl.pallas_call(functools.partial(field_kernel, sleepers, count, seglen, s...  56.7 us
    ppermute x6, starting transfers between devices, shift(): return lax.ppermute(array, axis, pairs)  18.3 us
    ppermute x6, waiting for transfers between devices, shift(): return lax.ppermute(array, axis, pairs)  7.63 us
    pallas_call x1, Pallas kernels, edges_of(): pl.pallas_call(functools.partial(edge_kernel, sleepers, spots), out_shape...  2.7 us
    ppermute x1, starting transfers between devices, local(): lax.ppermute(sleeper_pos, 'ka', turn)  2.04 us
  transfers between devices with their start and end apart: 9, of which 3 were waited for; matrix products, arithmetic and copies ran while one was open for 5% of the time, Pallas kernels for 1%

profile of v1, /device:TPU:1, one launch (start us, length us, event | category | flops | bytes accessed | tf_op | source)
XLA Modules:
  0.0 96.7 jit_solution(17112397885550001459)
XLA Ops:
  0.0 2.0 %collective-permute-start.2 = (s32[16]{0:T(128)}, s32[16]{0:T(128)S(1)}, u32[]{:S(2)}, u32[]{:S(2)}) collective-permute-start(s32[16]{0:T(128)} %param.5), channel_id=1, source_target_pairs={{0,16},{16,0},{1,17},{17,1},{2,18},{18,2},{3,19},{19,3},{4,20},{20... | collective-permute-start | bytes 200 | tf_op jit(solution)/shard_map/ppermute | solution.py:514
  2.0 1.1 %fusion.1 = (f32[48,8,128]{2,1,0:T(8,128)S(1)}, f32[48,8,128]{2,1,0:T(8,128)S(1)}) fusion(f32[48,32,128]{2,1,0:T(8,128)} %bitcast.6), kind=kLoop, calls=%fused_computation.14 | loop fusion | bytes 786432 | tf_op jit(solution)/shard_map/slice | solution.py:510
  3.1 0.1 collective-permute-start
  3.3 1.0 %slice.49 = f32[48,16,128]{2,1,0:T(8,128)S(1)} slice(f32[48,32,128]{2,1,0:T(8,128)} %bitcast.7), slice={[0:48], [8:24], [0:128]} | slice | bytes 786432 | tf_op jit(solution)/shard_map/slice | solution.py:512
  4.3 1.5 %collective-permute-start.5 = (f32[48,16,128]{2,1,0:T(8,128)S(1)}, f32[48,16,128]{2,1,0:T(8,128)S(1)}, u32[]{:S(2)}, u32[]{:S(2)}) collective-permute-start(f32[48,16,128]{2,1,0:T(8,128)S(1)} %slice.49), channel_id=1, source_target_pairs={{0,16},{16,0},{1,17},{17,1},{2,18},{18,2},{3,19},{19,3},{4,20},{20... | collective-permute-start | bytes 1179656 | tf_op jit(solution)/shard_map/ppermute | solution.py:513
  5.8 0.7 convert_bitcast_fusion.refs_1_.refs_8_
  6.5 0.1 and_select_fusion
  6.6 0.0 collective-permute-done.2
  6.6 0.7 pad_add_fusion
  7.3 0.1 broadcast_in_dim.24.positions
  7.4 0.7 copy-done.2
  8.1 0.9 tables.1
  9.0 1.1 %fusion = (f32[48,8,128]{2,1,0:T(8,128)S(1)}, f32[48,8,128]{2,1,0:T(8,128)S(1)}) fusion(f32[48,32,128]{2,1,0:T(8,128)} %bitcast.8), kind=kLoop, calls=%fused_computation.13 | loop fusion | bytes 786432 | tf_op jit(solution)/shard_map/slice | solution.py:519
  10.1 3.2 %collective-permute-start.3 = (f32[49,8,128]{2,1,0:T(8,128)S(1)}, f32[49,8,128]{2,1,0:T(8,128)S(1)}, u32[]{:S(2)}, u32[]{:S(2)}) collective-permute-start(f32[49,8,128]{2,1,0:T(8,128)S(1)} %pad_maximum_fusion.1), channel_id=1, source_target_pairs={{0,4},{4,8},{8,12},{1,5},{5,9},{9,13},{2,6},{6,10},{10,14},{3,7},{... | collective-permute-start | bytes 602120 | tf_op jit(solution)/shard_map/ppermute | solution.py:507
  13.3 1.3 %collective-permute-start.4 = (f32[49,8,128]{2,1,0:T(8,128)S(1)}, f32[49,8,128]{2,1,0:T(8,128)S(1)}, u32[]{:S(2)}, u32[]{:S(2)}) collective-permute-start(f32[49,8,128]{2,1,0:T(8,128)S(1)} %pad_maximum_fusion.2), channel_id=1, source_target_pairs={{4,0},{8,4},{12,8},{5,1},{9,5},{13,9},{6,2},{10,6},{14,10},{7,3},{... | collective-permute-start | bytes 602120 | tf_op jit(solution)/shard_map/ppermute | solution.py:507
  14.6 0.0 collective-permute-done.refs_4_.refs_11_
  14.6 4.0 %collective-permute-start.6 = (f32[48,8,128]{2,1,0:T(8,128)S(1)}, f32[48,8,128]{2,1,0:T(8,128)S(1)}, u32[]{:S(2)}, u32[]{:S(2)}) collective-permute-start(f32[48,8,128]{2,1,0:T(8,128)S(1)} %get-tuple-element.31), channel_id=1, source_target_pairs={{0,4},{4,8},{8,12},{1,5},{5,9},{9,13},{2,6},{6,10},{10,14},{3,7},{... | collective-permute-start | bytes 589832 | tf_op jit(solution)/shard_map/ppermute | solution.py:507
  18.7 1.3 %collective-permute-start.1 = (f32[48,8,128]{2,1,0:T(8,128)S(1)}, f32[48,8,128]{2,1,0:T(8,128)S(1)}, u32[]{:S(2)}, u32[]{:S(2)}) collective-permute-start(f32[48,8,128]{2,1,0:T(8,128)S(1)} %get-tuple-element.32), channel_id=1, source_target_pairs={{4,0},{8,4},{12,8},{5,1},{9,5},{13,9},{6,2},{10,6},{14,10},{7,3},{... | collective-permute-start | bytes 589832 | tf_op jit(solution)/shard_map/ppermute | solution.py:507
  20.0 0.1 add_convert_fusion.refs_0_
  20.0 5.0 %collective-permute-done.1.refs_7_.refs_14_ = f32[48,8,128]{2,1,0:T(8,128)S(1)} collective-permute-done((f32[48,8,128]{2,1,0:T(8,128)S(1)}, f32[48,8,128]{2,1,0:T(8,128)S(1)}, u32[]{:S(2)}, u32[]{:S(2)}) %collective-permute-start.1) | collective-permute-done | bytes 196640 | tf_op jit(solution)/shard_map/ppermute | solution.py:507
  25.1 0.0 collective-permute-done.3.refs_2_.refs_9_
  25.1 0.0 collective-permute-done.4.refs_3_.refs_10_
  25.1 0.0 collective-permute-done.5.refs_5_.refs_12_
  25.1 0.0 collective-permute-done.6.refs_6_.refs_13_
  25.1 0.0 copy-start
  25.1 1.1 %copy-done = f32[16,3,32,128]{3,2,1,0:T(8,128)S(1)} copy-done((f32[16,3,32,128]{3,2,1,0:T(8,128)S(1)}, f32[16,3,32,128]{3,2,1,0:T(8,128)}, u32[]{:S(2)}) %copy-start) | copy-done | bytes 786456
  26.2 2.7 %edge_columns.1 = f32[48,16,128]{2,1,0:T(8,128)S(1)} custom-call(f32[48,32,128]{2,1,0:T(8,128)S(1)} %bitcast.9, f32[1,32,128]{2,1,0:T(8,128)S(1)} %convert_bitcast_fusion.refs_1_.refs_8_, f32[49,8,128]{2,1,0:T(8,128)S(1)} %collective-permute-done.3.refs_2_.refs_9_, f32[49,8,128]{2,1,0:T(8,128)S(1)} %collective-permute-done.4.refs_3_.refs_10_, ...), custom_call_target="tpu_custom_call" | custom-call | tf_op jit(solution)/shard_map/edge_columns/pallas_call | solution.py:166
  29.0 5.4 %collective-permute-start.8 = (f32[48,8,128]{2,1,0:T(8,128)S(1)}, f32[48,8,128]{2,1,0:T(8,128)S(1)}, u32[]{:S(2)}, u32[]{:S(2)}) collective-permute-start(f32[48,8,128]{2,1,0:T(8,128)S(1)} %get-tuple-element.29), channel_id=1, source_target_pairs={{1,0},{2,1},{3,2},{5,4},{6,5},{7,6},{9,8},{10,9},{11,10},{13,12},{... | collective-permute-start | bytes 589832 | tf_op jit(solution)/shard_map/ppermute | solution.py:507
  34.4 3.0 %collective-permute-start.7 = (f32[48,8,128]{2,1,0:T(8,128)S(1)}, f32[48,8,128]{2,1,0:T(8,128)S(1)}, u32[]{:S(2)}, u32[]{:S(2)}) collective-permute-start(f32[48,8,128]{2,1,0:T(8,128)S(1)} %get-tuple-element.30), channel_id=1, source_target_pairs={{0,1},{1,2},{2,3},{4,5},{5,6},{6,7},{8,9},{9,10},{10,11},{12,13},{... | collective-permute-start | bytes 589832 | tf_op jit(solution)/shard_map/ppermute | solution.py:507
  37.5 1.4 %collective-permute-done.8.refs_2_ = f32[48,8,128]{2,1,0:T(8,128)S(1)} collective-permute-done((f32[48,8,128]{2,1,0:T(8,128)S(1)}, f32[48,8,128]{2,1,0:T(8,128)S(1)}, u32[]{:S(2)}, u32[]{:S(2)}) %collective-permute-start.8) | collective-permute-done | bytes 196640 | tf_op jit(solution)/shard_map/ppermute | solution.py:507
  38.9 1.2 %collective-permute-done.7.refs_1_ = f32[48,8,128]{2,1,0:T(8,128)S(1)} collective-permute-done((f32[48,8,128]{2,1,0:T(8,128)S(1)}, f32[48,8,128]{2,1,0:T(8,128)S(1)}, u32[]{:S(2)}, u32[]{:S(2)}) %collective-permute-start.7) | collective-permute-done | bytes 196640 | tf_op jit(solution)/shard_map/ppermute | solution.py:507
  40.0 56.7 %adjoint_field.1 = f32[64,2,3,32,128]{4,3,2,1,0:T(8,128)} custom-call(s32[2]{0:T(128)S(1)} %add_convert_fusion.refs_0_, f32[48,8,128]{2,1,0:T(8,128)S(1)} %collective-permute-done.7.refs_1_, f32[48,8,128]{2,1,0:T(8,128)S(1)} %collective-permute-done.8.refs_2_, bf16[768,768]{1,0:T(8,128)(2,1)S(1)} %get-tuple-element.21.refs_3_, ...), custom_call_target="tpu_custom_call" | custom-call | tf_op jit(solution)/shard_map/adjoint_field/pallas_call | solution.py:480
  (14 shorter events, 0.2 us)
Async XLA Ops:
  0.0 40.0 %copy-start.1 = (f32[16,3,32,128]{3,2,1,0:T(8,128)S(1)}, f32[16,3,32,128]{3,2,1,0:T(8,128)}, u32[]{:S(2)}) copy-start(f32[16,3,32,128]{3,2,1,0:T(8,128)} %param.4) | copy-start | bytes 2359300
  0.0 6.6 %collective-permute-start.2 = (s32[16]{0:T(128)}, s32[16]{0:T(128)S(1)}, u32[]{:S(2)}, u32[]{:S(2)}) collective-permute-start(s32[16]{0:T(128)} %param.5), channel_id=1, source_target_pairs={{0,16},{16,0},{1,17},{17,1},{2,18},{18,2},{3,19},{19,3},{4,20},{20... | collective-permute-start | bytes 200 | tf_op jit(solution)/shard_map/ppermute | solution.py:514
  3.1 11.5 %collective-permute-start = (f32[48,16,128]{2,1,0:T(8,128)S(1)}, f32[48,16,128]{2,1,0:T(8,128)S(1)}, u32[]{:S(2)}, u32[]{:S(2)}) collective-permute-start(f32[48,16,128]{2,1,0:T(8,128)S(1)} %pad_maximum_fusion), channel_id=1, source_target_pairs={{0,16},{16,0},{1,17},{17,1},{2,18},{18,2},{3,19},{19,3},{4,20},{20... | collective-permute-start | bytes 1179656 | tf_op jit(solution)/shard_map/ppermute | solution.py:511
  4.3 20.8 %collective-permute-start.5 = (f32[48,16,128]{2,1,0:T(8,128)S(1)}, f32[48,16,128]{2,1,0:T(8,128)S(1)}, u32[]{:S(2)}, u32[]{:S(2)}) collective-permute-start(f32[48,16,128]{2,1,0:T(8,128)S(1)} %slice.49), channel_id=1, source_target_pairs={{0,16},{16,0},{1,17},{17,1},{2,18},{18,2},{3,19},{19,3},{4,20},{20... | collective-permute-start | bytes 1179656 | tf_op jit(solution)/shard_map/ppermute | solution.py:513
  7.4 0.7 copy-start.2
  10.1 15.0 %collective-permute-start.3 = (f32[49,8,128]{2,1,0:T(8,128)S(1)}, f32[49,8,128]{2,1,0:T(8,128)S(1)}, u32[]{:S(2)}, u32[]{:S(2)}) collective-permute-start(f32[49,8,128]{2,1,0:T(8,128)S(1)} %pad_maximum_fusion.1), channel_id=1, source_target_pairs={{0,4},{4,8},{8,12},{1,5},{5,9},{9,13},{2,6},{6,10},{10,14},{3,7},{... | collective-permute-start | bytes 602120 | tf_op jit(solution)/shard_map/ppermute | solution.py:507
  13.3 11.8 %collective-permute-start.4 = (f32[49,8,128]{2,1,0:T(8,128)S(1)}, f32[49,8,128]{2,1,0:T(8,128)S(1)}, u32[]{:S(2)}, u32[]{:S(2)}) collective-permute-start(f32[49,8,128]{2,1,0:T(8,128)S(1)} %pad_maximum_fusion.2), channel_id=1, source_target_pairs={{4,0},{8,4},{12,8},{5,1},{9,5},{13,9},{6,2},{10,6},{14,10},{7,3},{... | collective-permute-start | bytes 602120 | tf_op jit(solution)/shard_map/ppermute | solution.py:507
  14.6 10.4 %collective-permute-start.6 = (f32[48,8,128]{2,1,0:T(8,128)S(1)}, f32[48,8,128]{2,1,0:T(8,128)S(1)}, u32[]{:S(2)}, u32[]{:S(2)}) collective-permute-start(f32[48,8,128]{2,1,0:T(8,128)S(1)} %get-tuple-element.31), channel_id=1, source_target_pairs={{0,4},{4,8},{8,12},{1,5},{5,9},{9,13},{2,6},{6,10},{10,14},{3,7},{... | collective-permute-start | bytes 589832 | tf_op jit(solution)/shard_map/ppermute | solution.py:507
  18.7 6.4 %collective-permute-start.1 = (f32[48,8,128]{2,1,0:T(8,128)S(1)}, f32[48,8,128]{2,1,0:T(8,128)S(1)}, u32[]{:S(2)}, u32[]{:S(2)}) collective-permute-start(f32[48,8,128]{2,1,0:T(8,128)S(1)} %get-tuple-element.32), channel_id=1, source_target_pairs={{4,0},{8,4},{12,8},{5,1},{9,5},{13,9},{6,2},{10,6},{14,10},{7,3},{... | collective-permute-start | bytes 589832 | tf_op jit(solution)/shard_map/ppermute | solution.py:507
  25.1 1.1 %copy-start = (f32[16,3,32,128]{3,2,1,0:T(8,128)S(1)}, f32[16,3,32,128]{3,2,1,0:T(8,128)}, u32[]{:S(2)}) copy-start(f32[16,3,32,128]{3,2,1,0:T(8,128)} %param.4) | copy-start | bytes 2359300
  29.0 9.9 %collective-permute-start.8 = (f32[48,8,128]{2,1,0:T(8,128)S(1)}, f32[48,8,128]{2,1,0:T(8,128)S(1)}, u32[]{:S(2)}, u32[]{:S(2)}) collective-permute-start(f32[48,8,128]{2,1,0:T(8,128)S(1)} %get-tuple-element.29), channel_id=1, source_target_pairs={{1,0},{2,1},{3,2},{5,4},{6,5},{7,6},{9,8},{10,9},{11,10},{13,12},{... | collective-permute-start | bytes 589832 | tf_op jit(solution)/shard_map/ppermute | solution.py:507
  34.4 5.6 %collective-permute-start.7 = (f32[48,8,128]{2,1,0:T(8,128)S(1)}, f32[48,8,128]{2,1,0:T(8,128)S(1)}, u32[]{:S(2)}, u32[]{:S(2)}) collective-permute-start(f32[48,8,128]{2,1,0:T(8,128)S(1)} %get-tuple-element.30), channel_id=1, source_target_pairs={{0,1},{1,2},{2,3},{4,5},{5,6},{6,7},{8,9},{9,10},{10,11},{12,13},{... | collective-permute-start | bytes 589832 | tf_op jit(solution)/shard_map/ppermute | solution.py:507
